TPU v7x, 256 devices: a whole 4x4x8 slice. The times are simulated.
256 devices in a mesh: kvp: 32 (over y, z), head: 8 (over x, core).
Axes of the slice: x: 4, y: 4, z: 8, core: 2. Of those that a mesh axis runs over, the one named last changes fastest.
Arguments:
- queries: bfloat16 [2, 128, 128], P(None, 'head'), may hold values from -200 to 200
- key_cache: bfloat16 [2, 8, 16384, 128], P(None, 'head', 'kvp'), may hold values from -6 to 6
- value_cache: bfloat16 [2, 8, 16384, 128], P(None, 'head', 'kvp'), may hold values from -6 to 6
- new_key: bfloat16 [2, 8, 128], P(None, 'head'), may hold values from -6 to 6
- new_value: bfloat16 [2, 8, 128], P(None, 'head'), may hold values from -6 to 6
- lengths: int32 [2], replicated, may hold values from 8192 to 16384, as said below
- residual_in: bfloat16 [2, 16384], P(None, ('kvp', 'head')), may hold values from -6 to 6
- out_weight: bfloat16 [16384, 16384], P('head', 'kvp'), may hold values from -0.09375 to 0.09375
- norm_gain: float32 [16384], P(('kvp', 'head')), may hold values from 0.1 to 1.9
- gate_weight: bfloat16 [26624, 16384], P(('kvp', 'head')), may hold values from -0.046875 to 0.046875
- up_weight: bfloat16 [26624, 16384], P(('kvp', 'head')), may hold values from -0.046875 to 0.046875
- down_weight: bfloat16 [26624, 16384], P(('kvp', 'head')), may hold values from -0.15625 to 0.15625
Outputs:
- layer_out: bfloat16 [2, 16384], P(None, ('kvp', 'head'))
Inputs may be any that keep to these rules, and one draw needn't show every extreme that they name: `lengths`: one of the two sequences has exactly 16384 cached tokens, the other at least 8192.
All inputs are finite; a program needn't handle non-finite values.
Results may differ from a plain program's by a relative error of at most 0.017.
Values may be sent and summed in bfloat16 or wider, within the bound.
A program may use at most 64 MiB of HBM per device.

v0:
```python
import jax
import jax.numpy as jnp
from jax import lax
from jax.sharding import PartitionSpec as P

D = 16384


epsilon = 1e-05


def by_rows(normed, weight_rows):
    return lax.dot_general(
        normed, weight_rows, (((1,), (1,)), ((), ())), preferred_element_type=jnp.float32
    )


def per_device(
    queries,
    key_cache,
    value_cache,
    new_key,
    new_value,
    lengths,
    residual_in,
    out_weight,
    norm_gain,
    gate_weight,
    up_weight,
    down_weight,
):
    seq_count, local_heads, head_dim = queries.shape
    groups = key_cache.shape[1]
    tokens_here = key_cache.shape[2]
    scale = 1.0 / head_dim**0.5
    grouped = queries.reshape(seq_count, groups, local_heads // groups, head_dim)
    scores = (
        jnp.einsum("bghd,bgtd->bght", grouped, key_cache, preferred_element_type=jnp.float32)
        * scale
    )
    positions = lax.axis_index("kvp") * tokens_here + jnp.arange(tokens_here, dtype=jnp.int32)
    in_range = (positions[None, :] < lengths[:, None])[:, None, None, :]
    scores = jnp.where(in_range, scores, -1e30)
    local_top = jnp.max(scores, axis=-1)
    weights = jnp.where(in_range, jnp.exp(scores - local_top[..., None]), 0.0)
    local_sum = jnp.sum(weights, axis=-1)
    local_acc = jnp.einsum(
        "bght,bgtd->bghd",
        weights.astype(jnp.bfloat16),
        value_cache,
        preferred_element_type=jnp.float32,
    )
    top_score = lax.pmax(local_top, "kvp")
    factor = jnp.exp(local_top - top_score)
    weight_sum, weighted = lax.psum((local_sum * factor, local_acc * factor[..., None]), "kvp")
    fresh = (
        jnp.einsum("bghd,bgd->bgh", grouped, new_key, preferred_element_type=jnp.float32) * scale
    )
    final_top = jnp.maximum(top_score, fresh)
    carried = jnp.exp(top_score - final_top)
    fresh_weight = jnp.exp(fresh - final_top)
    weight_sum = weight_sum * carried + fresh_weight
    weighted = (
        weighted * carried[..., None]
        + fresh_weight.astype(jnp.bfloat16).astype(jnp.float32)[..., None]
        * new_value.astype(jnp.float32)[:, :, None, :]
    )
    attended = (
        (weighted / weight_sum[..., None])
        .astype(jnp.bfloat16)
        .reshape(seq_count, local_heads * head_dim)
    )
    projected = jnp.dot(attended, out_weight, preferred_element_type=jnp.float32)
    stream = residual_in.astype(jnp.float32) + lax.psum_scatter(
        projected, "head", scatter_dimension=1, tiled=True
    )
    square_total = lax.psum(jnp.sum(stream * stream, axis=1), ("kvp", "head"))
    scaled = stream * lax.rsqrt(square_total / D + epsilon)[:, None] * norm_gain[None, :]
    normed = lax.all_gather(scaled.astype(jnp.bfloat16), ("kvp", "head"), axis=1, tiled=True)
    gate_act = by_rows(normed, gate_weight)
    up_act = by_rows(normed, up_weight)
    hidden = (jax.nn.silu(gate_act) * up_act).astype(jnp.bfloat16)
    partial_out = jnp.dot(hidden, down_weight, preferred_element_type=jnp.float32)
    feed_out = lax.psum_scatter(partial_out, ("kvp", "head"), scatter_dimension=1, tiled=True)
    return (stream + feed_out).astype(jnp.bfloat16)


def solution(mesh):
    in_specs = (
        P(None, "head", None),
        P(None, "head", "kvp", None),
        P(None, "head", "kvp", None),
        P(None, "head", None),
        P(None, "head", None),
        P(),
        P(None, ("kvp", "head")),
        P("head", "kvp"),
        P(("kvp", "head")),
        P(("kvp", "head"), None),
        P(("kvp", "head"), None),
        P(("kvp", "head"), None),
    )
    out_specs = P(None, ("kvp", "head"))
    return jax.shard_map(
        per_device, mesh=mesh, in_specs=in_specs, out_specs=out_specs, check_vma=False
    )
```

profile of v0, /device:TPU:1, one launch (start us, length us, event | category | flops | bytes accessed | tf_op | source)
XLA Modules:
  0.0 1680.7 jit_solution(1311945763355688177)
XLA Ops:
  6.5 0.0 copy-start
  6.5 0.0 copy-start.2
  6.5 0.0 reduce-scatter.7.cloned.1.call-start
  6.6 0.8 bitcast_convert_fusion
  7.4 1.0 fusion.16
  8.3 0.7 broadcast_compare_fusion
  9.1 1.2 fusion.27
  10.3 64.6 %pmax.7 = f32[2,1,16]{2,0,1:T(2,128)S(1)} all-reduce(f32[2,1,16]{2,0,1:T(2,128)S(1)} %bitcast.71), channel_id=1, replica_groups=mesh['kvp'=32,'head'=8] {'kvp'}, use_global_device_ids=true, to_apply=%region_1.2 | all-reduce | flops 32 | bytes 256 | tf_op jit(solution)/shard_map/pmax | solution.py:53
  74.9 0.2 fusion.5
  75.1 1.2 fusion.1
  76.2 110.5 %all-reduce = (f32[2,1,16]{2,0,1:T(2,128)S(1)}, f32[2,1,16,128]{3,2,0,1:T(8,128)S(1)}) all-reduce(f32[2,1,16]{2,0,1:T(2,128)S(1)} %get-tuple-element.11, f32[2,1,16,128]{3,2,0,1:T(8,128)S(1)} %fusion.1), channel_id=1, replica_groups=mesh['kvp'=32,'head'=8] {'kvp'}, use_global_device_ids=true, to_apply=%region_4.5 | all-reduce | flops 4128 | bytes 33024 | tf_op jit(solution)/shard_map/psum | solution.py:55
  186.8 0.1 fusion.13
  186.9 3.2 convolution_bitcast_fusion.1
  190.1 0.0 reduce-scatter.7.cloned.1.call-update
  190.1 0.0 reduce-scatter.9.cloned.1.call-start
  190.2 65.8 %reduce-scatter.7.cloned.1.call-done = f32[64,2]{1,0:T(8,128)} async-done(((f32[512,2]{1,0:T(8,128)}), f32[64,2]{1,0:T(8,128)}) %reduce-scatter.7.cloned.1.call-update) | async-done | bytes 528
  256.0 0.8 copy.18
  256.9 0.0 copy-done.2
  256.9 0.1 multiply_reduce_fusion
  257.0 78.4 %psum.23 = f32[2]{0:T(128)S(1)} all-reduce(f32[2]{0:T(128)S(1)} %multiply_reduce_fusion), channel_id=1, replica_groups=mesh['kvp'=32,'head'=8] {'kvp','head'}, use_global_device_ids=true, to_apply=%region_7.8 | all-reduce | flops 2 | bytes 16 | tf_op jit(solution)/shard_map/psum | solution.py:77
  335.4 0.0 copy-done.3
  335.4 0.1 fusion.21
  335.5 54.0 %all-gather = bf16[256,64,2]{1,2,0:T(2,128)(2,1)S(1)} all-gather(bf16[1,64,2]{1,2,0:T(2,128)(2,1)S(1)} %fusion.21), channel_id=1, replica_groups=mesh['kvp'=32,'head'=8] {'kvp','head'}, dimensions={0}, use_global_device_ids=true | all-gather | bytes 65792 | tf_op jit(solution)/shard_map/all_gather | solution.py:79
  389.5 0.8 reshape.95
  390.3 3.0 fusion.28
  393.3 0.0 copy-done
  393.3 0.0 copy-done.1
  393.3 9.2 convolution_bitcast_fusion
  402.5 0.0 reduce-scatter.9.cloned.1.call-update
  402.5 1270.0 %reduce-scatter.9.cloned.1.call-done = f32[64,2]{1,0:T(8,128)} async-done(((f32[16384,2]{1,0:T(8,128)}), f32[64,2]{1,0:T(8,128)}) %reduce-scatter.9.cloned.1.call-update) | async-done | bytes 528
  1672.5 0.8 copy.20
  1673.4 0.5 add_convert_fusion
  (7 shorter events, 0.0 us)
Async XLA Ops:
  6.5 386.8 %copy-start = (bf16[104,16384]{1,0:T(8,128)(2,1)S(1)}, bf16[104,16384]{1,0:T(8,128)(2,1)}, u32[]{:S(2)}) copy-start(bf16[104,16384]{1,0:T(8,128)(2,1)} %param.23) | copy-start | bytes 10223620
  6.5 250.3 %copy-start.2 = (bf16[2,64]{1,0:T(2,128)(2,1)S(1)}, bf16[2,64]{1,0:T(2,128)(2,1)}, u32[]{:S(2)}) copy-start(bf16[2,64]{1,0:T(2,128)(2,1)} %param.18) | copy-start | bytes 772
  6.5 328.8 %copy-start.3 = (f32[64]{0:T(128)S(1)}, f32[64]{0:T(128)}, u32[]{:S(2)}) copy-start(f32[64]{0:T(128)} %param.20) | copy-start | bytes 772
  6.5 249.5 %reduce-scatter.7.cloned.1.call-start = ((), (), s32[]{:S(2)}) async-start(), calls=%async_computation.2 | async-start | bytes 294912
  190.1 1482.4 %reduce-scatter.9.cloned.1.call-start = ((), (), s32[]{:S(2)}) async-start(), calls=%async_computation.3 | async-start | bytes 8421376
  390.3 3.0 copy-start.1
Sparse Core Ops, SparseCore 0:
  190.3 65.7 reduce-scatter.6
  402.6 1269.8 reduce-scatter.8
where the time goes:
time: 1690 us; the launch traced here: 1680 us
  waiting for transfers between devices  1340 us (79%)
  blocking collectives  308 us (18%)
  matrix products  18.8 us (1%)
    unnamed x4, waiting for transfers between devices  1340 us
    psum x1, blocking collectives, per_device(): lax.psum((local_sum * factor, local_acc * factor[..., None]), 'kvp')  111 us
    psum x1, blocking collectives, per_device(): square_total = lax.psum(jnp.sum(stream * stream, axis=1), ('kvp', 'head'))  78.4 us
    pmax x1, blocking collectives, per_device(): top_score = lax.pmax(local_top, 'kvp')  64.6 us
    all_gather x1, blocking collectives, per_device(): lax.all_gather(scaled.astype(jnp.bfloat16), ('kvp', 'head'), axis=1, tile...  54 us
  transfers between devices with their start and end apart: 2, of which 2 were waited for; matrix products, arithmetic and copies ran while one was open for 0% of the time, Pallas kernels for 0%

commit v1 on v0

v1 whole, which is shorter than its diff:
```python
import jax
import jax.numpy as jnp
from jax import lax
from jax.experimental import pallas as pl
from jax.experimental.pallas import tpu as pltpu
from jax.sharding import PartitionSpec as P

MESH = pl.DeviceIdType.MESH
NT = (((1,), (1,)), ((), ()))
f32 = jnp.float32
bf16 = jnp.bfloat16
EPSILON = 1e-05
MASKED = -1e30

NX, NY, NZ, NC = 4, 4, 8, 2
KVP, HEAD = NY * NZ, NX * NC
SEQS, GROUP, HD, TOKENS = 2, 16, 128, 512
D = 16384
BLOCK = D // KVP
TILES = BLOCK // 128
UNITS = 104
SCALE = HD**-0.5


def far_first(g):
    return jnp.where(lax.rem(g, 2) == 1, 4 - (g + 1) // 2, 4 + g // 2)


def kernel(
    q_ref, k_hbm, v_hbm, nk_ref, nv_ref, len_ref, res_ref, wo_hbm, gain_ref, wg_hbm, wu_hbm, wd_hbm,
    out_ref,
    k_buf, v_buf, wo_buf, wg_buf, wu_buf, wd_buf,
    y_acc, y_stat, z_acc, z_stat, att_buf,
    gain_buf, e_send, e_buf, stream_buf, f_buf, h_send, h_buf, i_send, i_buf,
    local_sem, y_send_sem, y_recv_sem, z_send_sem, z_recv_sem, ys_send_sem, ys_recv_sem, zs_send_sem, zs_recv_sem,
    gain_send_sem, gain_recv_sem, e_send_sem, e_recv_sem, f_send_sem, f_recv_sem, h_send_sem, h_recv_sem,
    i_send_sem, i_recv_sem,
):
    kvp, head = lax.axis_index("kvp"), lax.axis_index("head")
    y, z = kvp // NZ, lax.rem(kvp, NZ)
    x, core = head // NC, lax.rem(head, NC)
    slot = z * NY + y

    def at_yz(yy, zz):
        return (yy * NZ + zz, head)

    def at_head(hh):
        return (kvp, hh)

    y_peers = [(at_yz(lax.rem(y + d, NY), z)) for d in (2, 1, 3)]
    z_peers = [(at_yz(y, lax.rem(z + d, NZ))) for d in (4, 3, 5, 2, 6, 1, 7)]
    head_offsets = [(2, 1), (2, 0), (1, 1), (3, 1), (1, 0), (3, 0), (0, 1)]
    head_peers = [lax.rem(x + dx, NX) * NC + lax.rem(core + dc, NC) for dx, dc in head_offsets]

    barrier = pltpu.get_barrier_semaphore()
    greeted = z_peers + [at_head(hh) for hh in head_peers] + y_peers
    for peer in greeted:
        pl.semaphore_signal(barrier, inc=1, device_id=peer, device_id_type=MESH)

    loads = []
    for b in range(SEQS):
        loads.append(pltpu.make_async_copy(k_hbm.at[b, 0], k_buf.at[b], local_sem.at[b]))
        loads.append(pltpu.make_async_copy(v_hbm.at[b, 0], v_buf.at[b], local_sem.at[2 + b]))
    load_wo = pltpu.make_async_copy(wo_hbm, wo_buf, local_sem.at[4])
    load_wg = pltpu.make_async_copy(wg_hbm, wg_buf, local_sem.at[5])
    load_wu = pltpu.make_async_copy(wu_hbm, wu_buf, local_sem.at[6])
    load_wd = pltpu.make_async_copy(wd_hbm, wd_buf, local_sem.at[7])
    for load in loads + [load_wo, load_wg, load_wu, load_wd]:
        load.start()

    def put(src, dst, send_sem, recv_sem, peer):
        pltpu.make_async_remote_copy(
            src_ref=src, dst_ref=dst, send_sem=send_sem, recv_sem=recv_sem, device_id=peer, device_id_type=MESH
        ).start()

    def drain(ref, sem):
        pltpu.make_async_copy(ref, ref, sem).wait()

    lane = lax.broadcasted_iota(jnp.int32, (1, 128), 1)
    lane16 = lax.rem(lane, GROUP)
    lane_group = lane // GROUP
    diagonal = lax.broadcasted_iota(jnp.int32, (GROUP, 128), 0) == lax.rem(
        lax.broadcasted_iota(jnp.int32, (GROUP, 128), 1), GROUP
    )
    my_half = (lane // 64) == core

    def to_row(column):
        return jnp.sum(jnp.where(diagonal, column, 0.0), axis=0, keepdims=True)

    gain_mine = jnp.reshape(gain_ref[...], (1, 64))
    gain_buf[head] = jnp.where(my_half, jnp.concatenate([gain_mine, gain_mine], axis=1), 0.0)

    def local_attention(b):
        q = q_ref[b]
        loads[2 * b].wait()
        scores = lax.dot_general(q, k_buf[b], NT, preferred_element_type=f32) * SCALE
        positions = kvp * TOKENS + lax.broadcasted_iota(jnp.int32, (GROUP, TOKENS), 1)
        in_range = positions < len_ref[b]
        scores = jnp.where(in_range, scores, MASKED)
        first = kvp == 0
        fresh = jnp.sum(q.astype(f32) * nk_ref[b].astype(f32), axis=1, keepdims=True) * SCALE
        fresh = jnp.where(first, fresh, MASKED)
        top = jnp.maximum(jnp.max(scores, axis=1, keepdims=True), fresh)
        weights = jnp.where(in_range, jnp.exp(scores - top), 0.0)
        fresh_weight = jnp.where(first, jnp.exp(fresh - top), 0.0)
        total = jnp.sum(weights, axis=1, keepdims=True) + fresh_weight
        loads[2 * b + 1].wait()
        acc = jnp.dot(weights.astype(bf16), v_buf[b], preferred_element_type=f32)
        acc = acc + fresh_weight.astype(bf16).astype(f32) * nv_ref[b].astype(f32)
        return acc, to_row(top), to_row(total)

    def send_y(b, acc, top, total):
        y_acc[b, y] = acc.astype(bf16)
        y_stat[b, y] = jnp.concatenate([top, total], axis=0)
        for peer in y_peers:
            put(y_stat.at[b, y], y_stat.at[b, y], ys_send_sem.at[b], ys_recv_sem.at[b], peer)
            put(y_acc.at[b, y], y_acc.at[b, y], y_send_sem.at[b], y_recv_sem.at[b], peer)

    def send_z(b, acc, top, total):
        z_acc[b, z] = acc.astype(bf16)
        z_stat[b, z] = jnp.concatenate([top, total], axis=0)
        for peer in z_peers:
            put(z_stat.at[b, z], z_stat.at[b, z], zs_send_sem.at[b], zs_recv_sem.at[b], peer)
            put(z_acc.at[b, z], z_acc.at[b, z], z_send_sem.at[b], z_recv_sem.at[b], peer)

    def merge(n, b, acc_buf, stat_buf, acc_sem, stat_sem, last):
        drain(stat_buf.at[b, pl.ds(0, n - 1)], stat_sem.at[b])
        tops = [stat_buf[b, s, 0:1, :] for s in range(n)]
        totals = [stat_buf[b, s, 1:2, :] for s in range(n)]
        top = tops[0]
        for t in tops[1:]:
            top = jnp.maximum(top, t)
        total = jnp.zeros((1, 128), f32)
        chosen = jnp.zeros((1, 128), f32)
        for s in range(n):
            factor = jnp.exp(tops[s] - top)
            total = total + totals[s] * factor
            chosen = jnp.where(lane_group == s, factor, chosen)
        if last:
            chosen = chosen / total
        spread = jnp.where(diagonal, chosen, 0.0).astype(bf16)
        drain(acc_buf.at[b, pl.ds(0, n - 1)], acc_sem.at[b])
        stacked = acc_buf[b].reshape(n * GROUP, HD)
        acc = jnp.dot(spread[:, : n * GROUP], stacked, preferred_element_type=f32)
        return acc, top, total

    part0 = local_attention(0)
    part1 = local_attention(1)

    pl.semaphore_wait(barrier, len(greeted))
    send_y(0, *part0)
    send_z(1, *part1)
    for hh in head_peers:
        put(gain_buf.at[head], gain_buf.at[head], gain_send_sem, gain_recv_sem, at_head(hh))

    send_z(0, *merge(NY, 0, y_acc, y_stat, y_recv_sem, ys_recv_sem, False))
    send_y(1, *merge(NZ, 1, z_acc, z_stat, z_recv_sem, zs_recv_sem, False))
    att_buf[0] = merge(NZ, 0, z_acc, z_stat, z_recv_sem, zs_recv_sem, True)[0]
    att_buf[1] = merge(NY, 1, y_acc, y_stat, y_recv_sem, ys_recv_sem, True)[0]

    attended = jnp.concatenate([att_buf[:, h, :] for h in range(GROUP)], axis=1).astype(bf16)
    load_wo.wait()
    projected = jnp.dot(attended, wo_buf[...], preferred_element_type=f32)
    residual = res_ref[...].astype(f32)
    residual = jnp.where(my_half, jnp.concatenate([residual, residual], axis=1), 0.0)
    for t in range(TILES):
        e_buf[head, t] = projected[:, t * 128 : (t + 1) * 128] + jnp.where(x == t, residual, 0.0)
    for hh in head_peers:
        put(e_buf.at[head], e_buf.at[head], e_send_sem, e_recv_sem, at_head(hh))
    drain(gain_buf.at[pl.ds(0, HEAD - 1)], gain_recv_sem)
    gains = [gain_buf[2 * t] + gain_buf[2 * t + 1] for t in range(TILES)]
    drain(e_buf.at[pl.ds(0, HEAD - 1)], e_recv_sem)
    squares = jnp.zeros((SEQS, 128), f32)
    for t in range(TILES):
        stream = e_buf[0, t]
        for hh in range(1, HEAD):
            stream = stream + e_buf[hh, t]
        stream_buf[t] = stream
        squares = squares + stream * stream
        f_buf[slot, t] = (stream * gains[t]).astype(bf16)
    square = jnp.sum(squares, axis=1, keepdims=True)
    piece0 = square.astype(bf16).astype(f32)
    piece1 = (square - piece0).astype(bf16).astype(f32)
    piece2 = square - piece0 - piece1
    f_buf[slot, TILES] = jnp.where(
        lane == 0, piece0, jnp.where(lane == 1, piece1, jnp.where(lane == 2, piece2, 0.0))
    ).astype(bf16)

    def send_f(peer):
        put(f_buf.at[slot], f_buf.at[slot], f_send_sem, f_recv_sem.at[z], peer)

    def send_f_group(g, carry):
        zz = lax.rem(z + far_first(g), NZ)
        for dy in (2, 1, 3, 0):
            send_f(at_yz(lax.rem(y + dy, NY), zz))
        return carry

    lax.fori_loop(0, NZ - 1, send_f_group, 0)
    for dy in (2, 1, 3):
        send_f(at_yz(lax.rem(y + dy, NY), z))

    load_wg.wait()
    load_wu.wait()

    def gate_up(zz, carry):
        gate, up, squares = carry
        for yy in range(NY):
            block = zz * NY + yy
            part = jnp.concatenate([f_buf[block, t] for t in range(TILES)], axis=1)
            columns = pl.ds(pl.multiple_of((yy * NZ + zz) * BLOCK, BLOCK), BLOCK)
            gate = gate + lax.dot_general(part, wg_buf[:, columns], NT, preferred_element_type=f32)
            up = up + lax.dot_general(part, wu_buf[:, columns], NT, preferred_element_type=f32)
            squares = squares + f_buf[block, TILES].astype(f32)
        return gate, up, squares

    zero = jnp.zeros((SEQS, UNITS), f32)
    drain(f_buf.at[pl.ds(0, NY - 1)], f_recv_sem.at[z])
    carry = gate_up(z, (zero, zero, jnp.zeros((SEQS, 128), f32)))

    def gate_up_group(i, carry):
        zz = lax.rem(z + far_first(NZ - 1 - i), NZ)
        drain(f_buf.at[pl.ds(0, NY)], f_recv_sem.at[zz])
        return gate_up(zz, carry)

    gate, up, squares = lax.fori_loop(1, NZ, gate_up_group, carry)
    factor = lax.rsqrt(jnp.sum(squares, axis=1, keepdims=True) / D + EPSILON)
    gate = gate * factor
    up = up * factor
    hidden = (gate / (1.0 + jnp.exp(-gate)) * up).astype(bf16)

    load_wd.wait()

    def down(yy, zz):
        block = zz * NY + yy
        columns = pl.ds(pl.multiple_of((yy * NZ + zz) * BLOCK, BLOCK), BLOCK)
        part = jnp.dot(hidden, wd_buf[:, columns], preferred_element_type=f32).astype(bf16)
        for t in range(TILES):
            h_send[block, t] = part[:, t * 128 : (t + 1) * 128]
        return block

    def send_h(yy, zz):
        block = zz * NY + yy
        put(h_send.at[block], h_buf.at[slot], h_send_sem, h_recv_sem, at_yz(yy, zz))

    def down_group(g, carry):
        zz = lax.rem(z + far_first(g), NZ)
        for dy in (2, 1, 3, 0):
            down(lax.rem(y + dy, NY), zz)
        for dy in (2, 1, 3, 0):
            send_h(lax.rem(y + dy, NY), zz)
        return carry

    lax.fori_loop(0, NZ - 1, down_group, 0)
    for dy in (2, 1, 3):
        down(lax.rem(y + dy, NY), z)
        send_h(lax.rem(y + dy, NY), z)
    down(y, z)
    for t in range(TILES):
        h_buf[slot, t] = h_send[slot, t]
    drain(h_buf.at[pl.ds(0, KVP - 1)], h_recv_sem)

    def add_block(s, sums):
        return tuple(sums[t] + h_buf[s, t].astype(f32) for t in range(TILES))

    sums = tuple(jnp.zeros((SEQS, 128), f32) for _ in range(TILES))
    sums = lax.fori_loop(0, KVP, add_block, sums, unroll=8)
    for t in range(TILES):
        i_send[t] = sums[t]

    for (dx, dc), hh in zip(head_offsets, head_peers):
        put(i_send.at[lax.rem(x + dx, NX)], i_buf.at[head], i_send_sem, i_recv_sem, at_head(hh))
    i_buf[head] = i_send[x]
    total = stream_buf[x]
    drain(i_buf.at[pl.ds(0, HEAD - 1)], i_recv_sem)
    for hh in range(HEAD):
        total = total + i_buf[hh]
    out_ref[...] = jnp.where(core == 0, total[:, :64], total[:, 64:]).astype(bf16)

    for b in range(SEQS):
        drain(y_acc.at[b, pl.ds(0, NY - 1)], y_send_sem.at[b])
        drain(y_stat.at[b, pl.ds(0, NY - 1)], ys_send_sem.at[b])
        drain(z_acc.at[b, pl.ds(0, NZ - 1)], z_send_sem.at[b])
        drain(z_stat.at[b, pl.ds(0, NZ - 1)], zs_send_sem.at[b])
    drain(gain_buf.at[pl.ds(0, HEAD - 1)], gain_send_sem)
    drain(e_buf.at[pl.ds(0, HEAD - 1)], e_send_sem)
    drain(f_buf.at[pl.ds(0, KVP - 1)], f_send_sem)
    drain(h_buf.at[pl.ds(0, KVP - 1)], h_send_sem)
    drain(i_buf.at[pl.ds(0, HEAD - 1)], i_send_sem)


def per_device(*args):
    vmem = pl.BlockSpec(memory_space=pltpu.VMEM)
    smem = pl.BlockSpec(memory_space=pltpu.SMEM)
    hbm = pl.BlockSpec(memory_space=pl.ANY)
    dma = pltpu.SemaphoreType.DMA
    return pl.pallas_call(
        kernel,
        out_shape=jax.ShapeDtypeStruct((SEQS, D // KVP // HEAD), bf16),
        in_specs=[vmem, hbm, hbm, vmem, vmem, smem, vmem, hbm, vmem, hbm, hbm, hbm],
        out_specs=vmem,
        scratch_shapes=[
            pltpu.VMEM((SEQS, TOKENS, HD), bf16),
            pltpu.VMEM((SEQS, TOKENS, HD), bf16),
            pltpu.VMEM((GROUP * HD, BLOCK), bf16),
            pltpu.VMEM((UNITS, D), bf16),
            pltpu.VMEM((UNITS, D), bf16),
            pltpu.VMEM((UNITS, D), bf16),
            pltpu.VMEM((SEQS, NY, GROUP, HD), bf16),
            pltpu.VMEM((SEQS, NY, 2, 128), f32),
            pltpu.VMEM((SEQS, NZ, GROUP, HD), bf16),
            pltpu.VMEM((SEQS, NZ, 2, 128), f32),
            pltpu.VMEM((SEQS, GROUP, HD), f32),
            pltpu.VMEM((HEAD, 1, 128), f32),
            pltpu.VMEM((TILES, SEQS, 128), f32),
            pltpu.VMEM((HEAD, TILES, SEQS, 128), f32),
            pltpu.VMEM((TILES, SEQS, 128), f32),
            pltpu.VMEM((KVP, TILES + 1, SEQS, 128), bf16),
            pltpu.VMEM((KVP, TILES, SEQS, 128), bf16),
            pltpu.VMEM((KVP, TILES, SEQS, 128), bf16),
            pltpu.VMEM((TILES, SEQS, 128), f32),
            pltpu.VMEM((HEAD, SEQS, 128), f32),
            dma((8,)),
            dma((SEQS,)), dma((SEQS,)), dma((SEQS,)), dma((SEQS,)),
            dma((SEQS,)), dma((SEQS,)), dma((SEQS,)), dma((SEQS,)),
            dma, dma, dma, dma, dma, dma((NZ,)), dma, dma, dma, dma,
        ],
        compiler_params=pltpu.CompilerParams(
            collective_id=0, has_side_effects=True, vmem_limit_bytes=32 * 1024 * 1024
        ),
        name="layer",
    )(*args)


def solution(mesh):
    in_specs = (
        P(None, "head", None),
        P(None, "head", "kvp", None),
        P(None, "head", "kvp", None),
        P(None, "head", None),
        P(None, "head", None),
        P(),
        P(None, ("kvp", "head")),
        P("head", "kvp"),
        P(("kvp", "head")),
        P(("kvp", "head"), None),
        P(("kvp", "head"), None),
        P(("kvp", "head"), None),
    )
    return jax.shard_map(
        per_device, mesh=mesh, in_specs=in_specs, out_specs=P(None, ("kvp", "head")), check_vma=False
    )
```

time: 1690 us -> 54.3 us (0.03)
  waiting for transfers between devices: 1340 us -> 0 us
  blocking collectives: 308 us -> 0 us
  Pallas kernels: 0 us -> 40 us
  matrix products: 18.8 us -> 0 us
    unnamed x4 -> x0, waiting for transfers between devices: 1340 us -> none
    psum x2 -> x0, blocking collectives: 189 us -> none  [the longest x1 111 us: per_device(): lax.psum((local_sum * factor, local_acc * factor[..., None]), 'kvp')]
    pmax x1 -> x0, blocking collectives: 64.6 us -> none  [per_device(): top_score = lax.pmax(local_top, 'kvp')]
    all_gather x1 -> x0, blocking collectives: 54 us -> none  [per_device(): lax.all_gather(scaled.astype(jnp.bfloat16), ('kvp', 'head'), axis=1, tile...]
    pallas_call x0 -> x1, Pallas kernels: none -> 40 us  [per_device(): pl.pallas_call(kernel, out_shape=jax.ShapeDtypeStruct((SEQS, D // KVP //...]
  transfers between devices with their start and end apart: 2 -> 0, of which waited for: 2 -> 0; matrix products, arithmetic and copies ran while one was open for 0% -> 0% of each run, Pallas kernels for 0% -> 0%
where the time goes in v1:
time: 54.3 us; the launch traced here: 53.9 us
  Pallas kernels  40 us (74%)
  local copies, waits for them, and re-layouts  13.9 us (26%)
    pallas_call x1, Pallas kernels, per_device(): pl.pallas_call(kernel, out_shape=jax.ShapeDtypeStruct((SEQS, D // KVP //...  40 us
    unnamed x23, local copies, waits for them, and re-layouts  13.9 us

profile of v1, /device:TPU:1, one launch (start us, length us, event | category | flops | bytes accessed | tf_op | source)
XLA Modules:
  0.0 53.9 jit_solution(4051274100671582203)
XLA Ops:
  0.0 0.7 %copy.13.nk_ref = bf16[2,1,128]{2,1,0:T(2,128)(2,1)S(1)} copy(bf16[2,1,128]{2,0,1:T(2,128)(2,1)} %param.15) | data formatting | bytes 1024 | tf_op args[3]
  0.7 0.7 %copy.14.nv_ref = bf16[2,1,128]{2,1,0:T(2,128)(2,1)S(1)} copy(bf16[2,1,128]{2,0,1:T(2,128)(2,1)} %param.16) | data formatting | bytes 1024 | tf_op args[4]
  1.3 0.0 copy-start
  1.3 2.0 %copy-done = bf16[104,16384]{1,0:T(8,128)(2,1)S(1)} copy-done((bf16[104,16384]{1,0:T(8,128)(2,1)S(1)}, bf16[104,16384]{1,0:T(8,128)(2,1)}, u32[]{:S(2)}) %copy-start) | copy-done | bytes 3407896
  3.3 0.0 copy-start.1
  3.3 2.0 %copy-done.1 = bf16[104,16384]{1,0:T(8,128)(2,1)S(1)} copy-done((bf16[104,16384]{1,0:T(8,128)(2,1)S(1)}, bf16[104,16384]{1,0:T(8,128)(2,1)}, u32[]{:S(2)}) %copy-start.1) | copy-done | bytes 3407896
  5.2 0.0 copy-start.2
  5.2 2.0 %copy-done.2 = bf16[104,16384]{1,0:T(8,128)(2,1)S(1)} copy-done((bf16[104,16384]{1,0:T(8,128)(2,1)S(1)}, bf16[104,16384]{1,0:T(8,128)(2,1)}, u32[]{:S(2)}) %copy-start.2) | copy-done | bytes 3407896
  7.2 0.0 copy-start.3
  7.2 1.6 %copy-done.3 = bf16[2048,512]{1,0:T(8,128)(2,1)S(1)} copy-done((bf16[2048,512]{1,0:T(8,128)(2,1)S(1)}, bf16[2048,512]{1,0:T(8,128)(2,1)}, u32[]{:S(2)}) %copy-start.3) | copy-done | bytes 2097176
  8.8 0.0 copy-start.4
  8.8 0.9 %copy-done.4 = bf16[2,1,512,128]{3,2,1,0:T(8,128)(2,1)S(1)} copy-done((bf16[2,1,512,128]{3,2,1,0:T(8,128)(2,1)S(1)}, bf16[2,1,512,128]{3,2,1,0:T(8,128)(2,1)}, u32[]{:S(2)}) %copy-start.4) | copy-done | bytes 262168
  9.8 0.0 copy-start.5
  9.8 0.9 %copy-done.5 = bf16[2,1,512,128]{3,2,1,0:T(8,128)(2,1)S(1)} copy-done((bf16[2,1,512,128]{3,2,1,0:T(8,128)(2,1)S(1)}, bf16[2,1,512,128]{3,2,1,0:T(8,128)(2,1)}, u32[]{:S(2)}) %copy-start.5) | copy-done | bytes 262168
  10.7 0.0 copy-start.6
  10.7 0.7 %copy-done.6 = bf16[2,16,128]{2,1,0:T(8,128)(2,1)S(1)} copy-done((bf16[2,16,128]{2,1,0:T(8,128)(2,1)S(1)}, bf16[2,16,128]{2,1,0:T(8,128)(2,1)}, u32[]{:S(2)}) %copy-start.6) | copy-done | bytes 8216
  11.4 0.0 copy-start.7
  11.4 0.7 %copy-done.7 = s32[2]{0:T(128)S(1)} copy-done((s32[2]{0:T(128)S(1)}, s32[2]{0:T(128)}, u32[]{:S(2)}) %copy-start.7) | copy-done | bytes 32
  12.1 0.0 copy-start.8
  12.1 0.7 %copy-done.8 = bf16[2,64]{1,0:T(2,128)(2,1)S(1)} copy-done((bf16[2,64]{1,0:T(2,128)(2,1)S(1)}, bf16[2,64]{1,0:T(2,128)(2,1)}, u32[]{:S(2)}) %copy-start.8) | copy-done | bytes 280
  12.7 0.0 copy-start.9
  12.7 0.7 %copy-done.9 = f32[64]{0:T(128)S(1)} copy-done((f32[64]{0:T(128)S(1)}, f32[64]{0:T(128)}, u32[]{:S(2)}) %copy-start.9) | copy-done | bytes 280
  13.4 40.0 %layer.1 = bf16[2,64]{1,0:T(2,128)(2,1)S(1)} custom-call(bf16[2,16,128]{2,1,0:T(8,128)(2,1)S(1)} %copy-done.6, bf16[2,1,512,128]{3,2,1,0:T(8,128)(2,1)S(1)} %copy-done.4, bf16[2,1,512,128]{3,2,1,0:T(8,128)(2,1)S(1)} %copy-done.5, bf16[2,1,128]{2,1,0:T(2,128)(2,1)S(1)} %copy.13.nk_ref, bf16[2,1,128]{2,1,0:T(2,128)(2,1)S(1)} %copy.14.nv_ref, s32[2]{0:T(128)S(1)} %copy-done.7, ...), custom_call_target="tpu_custom_call" | custom-call | tf_op jit(solution)/shard_map/layer/pallas_call | solution.py:296
  53.4 0.5 copy.16
Async XLA Ops:
  1.3 2.0 %copy-start = (bf16[104,16384]{1,0:T(8,128)(2,1)S(1)}, bf16[104,16384]{1,0:T(8,128)(2,1)}, u32[]{:S(2)}) copy-start(bf16[104,16384]{1,0:T(8,128)(2,1)} %wg_hbm.1) | copy-start | bytes 10223620
  3.3 2.0 %copy-start.1 = (bf16[104,16384]{1,0:T(8,128)(2,1)S(1)}, bf16[104,16384]{1,0:T(8,128)(2,1)}, u32[]{:S(2)}) copy-start(bf16[104,16384]{1,0:T(8,128)(2,1)} %wu_hbm.1) | copy-start | bytes 10223620
  5.2 2.0 %copy-start.2 = (bf16[104,16384]{1,0:T(8,128)(2,1)S(1)}, bf16[104,16384]{1,0:T(8,128)(2,1)}, u32[]{:S(2)}) copy-start(bf16[104,16384]{1,0:T(8,128)(2,1)} %wd_hbm.1) | copy-start | bytes 10223620
  7.2 1.6 %copy-start.3 = (bf16[2048,512]{1,0:T(8,128)(2,1)S(1)}, bf16[2048,512]{1,0:T(8,128)(2,1)}, u32[]{:S(2)}) copy-start(bf16[2048,512]{1,0:T(8,128)(2,1)} %wo_hbm.1) | copy-start | bytes 6291460
  8.8 0.9 %copy-start.4 = (bf16[2,1,512,128]{3,2,1,0:T(8,128)(2,1)S(1)}, bf16[2,1,512,128]{3,2,1,0:T(8,128)(2,1)}, u32[]{:S(2)}) copy-start(bf16[2,1,512,128]{3,2,1,0:T(8,128)(2,1)} %k_hbm.1) | copy-start | bytes 786436
  9.8 0.9 %copy-start.5 = (bf16[2,1,512,128]{3,2,1,0:T(8,128)(2,1)S(1)}, bf16[2,1,512,128]{3,2,1,0:T(8,128)(2,1)}, u32[]{:S(2)}) copy-start(bf16[2,1,512,128]{3,2,1,0:T(8,128)(2,1)} %v_hbm.1) | copy-start | bytes 786436
  10.7 0.7 %copy-start.6 = (bf16[2,16,128]{2,1,0:T(8,128)(2,1)S(1)}, bf16[2,16,128]{2,1,0:T(8,128)(2,1)}, u32[]{:S(2)}) copy-start(bf16[2,16,128]{2,1,0:T(8,128)(2,1)} %q_ref.1) | copy-start | bytes 24580
  11.4 0.7 %copy-start.7 = (s32[2]{0:T(128)S(1)}, s32[2]{0:T(128)}, u32[]{:S(2)}) copy-start(s32[2]{0:T(128)} %len_ref.1) | copy-start | bytes 28
  12.1 0.7 %copy-start.8 = (bf16[2,64]{1,0:T(2,128)(2,1)S(1)}, bf16[2,64]{1,0:T(2,128)(2,1)}, u32[]{:S(2)}) copy-start(bf16[2,64]{1,0:T(2,128)(2,1)} %res_ref.1) | copy-start | bytes 772
  12.7 0.7 %copy-start.9 = (f32[64]{0:T(128)S(1)}, f32[64]{0:T(128)}, u32[]{:S(2)}) copy-start(f32[64]{0:T(128)} %gain_ref.1) | copy-start | bytes 772

commit v2 on v1

--- a/solution.py
+++ b/solution.py
@@ -27,14 +27,15 @@
 
 
 def kernel(
-    q_ref, k_hbm, v_hbm, nk_ref, nv_ref, len_ref, res_ref, wo_hbm, gain_ref, wg_hbm, wu_hbm, wd_hbm,
+    q_hbm, k_hbm, v_hbm, nk_hbm, nv_hbm, len_hbm, res_hbm, wo_hbm, gain_hbm, wg_hbm, wu_hbm, wd_hbm,
     out_ref,
+    q_ref, nk_ref, nv_ref, len_ref, res_ref, gain_ref,
     k_buf, v_buf, wo_buf, wg_buf, wu_buf, wd_buf,
     y_acc, y_stat, z_acc, z_stat, att_buf,
-    gain_buf, e_send, e_buf, stream_buf, f_buf, h_send, h_buf, i_send, i_buf,
+    gain_buf, e_buf, stream_buf, f_buf, h_send, h_buf, i_send, i_buf,
     local_sem, y_send_sem, y_recv_sem, z_send_sem, z_recv_sem, ys_send_sem, ys_recv_sem, zs_send_sem, zs_recv_sem,
     gain_send_sem, gain_recv_sem, e_send_sem, e_recv_sem, f_send_sem, f_recv_sem, h_send_sem, h_recv_sem,
-    i_send_sem, i_recv_sem,
+    i_send_sem, i_recv_sem, small_sem,
 ):
     kvp, head = lax.axis_index("kvp"), lax.axis_index("head")
     y, z = kvp // NZ, lax.rem(kvp, NZ)
@@ -57,6 +58,15 @@
     for peer in greeted:
         pl.semaphore_signal(barrier, inc=1, device_id=peer, device_id_type=MESH)
 
+    smalls = [
+        pltpu.make_async_copy(src, dst, small_sem.at[i])
+        for i, (src, dst) in enumerate(
+            (
+                (q_hbm, q_ref), (nk_hbm, nk_ref), (nv_hbm, nv_ref), (len_hbm, len_ref), (res_hbm, res_ref),
+                (gain_hbm, gain_ref),
+            )
+        )
+    ]
     loads = []
     for b in range(SEQS):
         loads.append(pltpu.make_async_copy(k_hbm.at[b, 0], k_buf.at[b], local_sem.at[b]))
@@ -65,7 +75,7 @@
     load_wg = pltpu.make_async_copy(wg_hbm, wg_buf, local_sem.at[5])
     load_wu = pltpu.make_async_copy(wu_hbm, wu_buf, local_sem.at[6])
     load_wd = pltpu.make_async_copy(wd_hbm, wd_buf, local_sem.at[7])
-    for load in loads + [load_wo, load_wg, load_wu, load_wd]:
+    for load in smalls[:1] + loads + smalls[1:] + [load_wo, load_wg, load_wu, load_wd]:
         load.start()
 
     def put(src, dst, send_sem, recv_sem, peer):
@@ -86,6 +96,9 @@
 
     def to_row(column):
         return jnp.sum(jnp.where(diagonal, column, 0.0), axis=0, keepdims=True)
+
+    for small in smalls:
+        small.wait()
 
     gain_mine = jnp.reshape(gain_ref[...], (1, 64))
     gain_buf[head] = jnp.where(my_half, jnp.concatenate([gain_mine, gain_mine], axis=1), 0.0)
@@ -98,7 +111,7 @@
         in_range = positions < len_ref[b]
         scores = jnp.where(in_range, scores, MASKED)
         first = kvp == 0
-        fresh = jnp.sum(q.astype(f32) * nk_ref[b].astype(f32), axis=1, keepdims=True) * SCALE
+        fresh = jnp.sum(q.astype(f32) * nk_ref[b : b + 1, :].astype(f32), axis=1, keepdims=True) * SCALE
         fresh = jnp.where(first, fresh, MASKED)
         top = jnp.maximum(jnp.max(scores, axis=1, keepdims=True), fresh)
         weights = jnp.where(in_range, jnp.exp(scores - top), 0.0)
@@ -106,7 +119,7 @@
         total = jnp.sum(weights, axis=1, keepdims=True) + fresh_weight
         loads[2 * b + 1].wait()
         acc = jnp.dot(weights.astype(bf16), v_buf[b], preferred_element_type=f32)
-        acc = acc + fresh_weight.astype(bf16).astype(f32) * nv_ref[b].astype(f32)
+        acc = acc + fresh_weight.astype(bf16).astype(f32) * nv_ref[b : b + 1, :].astype(f32)
         return acc, to_row(top), to_row(total)
 
     def send_y(b, acc, top, total):
@@ -288,17 +301,23 @@
     drain(i_buf.at[pl.ds(0, HEAD - 1)], i_send_sem)
 
 
-def per_device(*args):
+def per_device(queries, key_cache, value_cache, new_key, new_value, *rest):
+    args = (queries, key_cache, value_cache, new_key.reshape(SEQS, HD), new_value.reshape(SEQS, HD)) + rest
     vmem = pl.BlockSpec(memory_space=pltpu.VMEM)
-    smem = pl.BlockSpec(memory_space=pltpu.SMEM)
-    hbm = pl.BlockSpec(memory_space=pl.ANY)
+    hbm = pl.BlockSpec(memory_space=pltpu.HBM)
     dma = pltpu.SemaphoreType.DMA
     return pl.pallas_call(
         kernel,
         out_shape=jax.ShapeDtypeStruct((SEQS, D // KVP // HEAD), bf16),
-        in_specs=[vmem, hbm, hbm, vmem, vmem, smem, vmem, hbm, vmem, hbm, hbm, hbm],
+        in_specs=[hbm] * 12,
         out_specs=vmem,
         scratch_shapes=[
+            pltpu.VMEM((SEQS, GROUP, HD), bf16),
+            pltpu.VMEM((SEQS, HD), bf16),
+            pltpu.VMEM((SEQS, HD), bf16),
+            pltpu.SMEM((SEQS,), jnp.int32),
+            pltpu.VMEM((SEQS, D // KVP // HEAD), bf16),
+            pltpu.VMEM((D // KVP // HEAD,), f32),
             pltpu.VMEM((SEQS, TOKENS, HD), bf16),
             pltpu.VMEM((SEQS, TOKENS, HD), bf16),
             pltpu.VMEM((GROUP * HD, BLOCK), bf16),
@@ -311,7 +330,6 @@
             pltpu.VMEM((SEQS, NZ, 2, 128), f32),
             pltpu.VMEM((SEQS, GROUP, HD), f32),
             pltpu.VMEM((HEAD, 1, 128), f32),
-            pltpu.VMEM((TILES, SEQS, 128), f32),
             pltpu.VMEM((HEAD, TILES, SEQS, 128), f32),
             pltpu.VMEM((TILES, SEQS, 128), f32),
             pltpu.VMEM((KVP, TILES + 1, SEQS, 128), bf16),
@@ -322,10 +340,10 @@
             dma((8,)),
             dma((SEQS,)), dma((SEQS,)), dma((SEQS,)), dma((SEQS,)),
             dma((SEQS,)), dma((SEQS,)), dma((SEQS,)), dma((SEQS,)),
-            dma, dma, dma, dma, dma, dma((NZ,)), dma, dma, dma, dma,
+            dma, dma, dma, dma, dma, dma((NZ,)), dma, dma, dma, dma, dma((6,)),
         ],
         compiler_params=pltpu.CompilerParams(
-            collective_id=0, has_side_effects=True, vmem_limit_bytes=32 * 1024 * 1024
+            collective_id=0, has_side_effects=True, vmem_limit_bytes=64 * 1024 * 1024
         ),
         name="layer",
     )(*args)

time: 54.3 us -> 43.2 us (0.80)
  local copies, waits for them, and re-layouts: 13.9 us -> 1.19 us
  Pallas kernels: 40 us -> 41.9 us
    unnamed x23 -> x1, local copies, waits for them, and re-layouts: 13.9 us -> 1.19 us
    pallas_call x1, Pallas kernels: 40 us -> 41.9 us  [per_device(): pl.pallas_call(kernel, out_shape=jax.ShapeDtypeStruct((SEQS, D // KVP //...]
where the time goes in v2:
time: 43.2 us; the launch traced here: 43.1 us
  Pallas kernels  41.9 us (97%)
  local copies, waits for them, and re-layouts  1.19 us (3%)
    pallas_call x1, Pallas kernels, per_device(): pl.pallas_call(kernel, out_shape=jax.ShapeDtypeStruct((SEQS, D // KVP //...  41.9 us
    unnamed x1, local copies, waits for them, and re-layouts  1.19 us

profile of v2, /device:TPU:1, one launch (start us, length us, event | category | flops | bytes accessed | tf_op | source)
XLA Modules:
  0.0 43.1 jit_solution(17657557958209291297)
XLA Ops:
  0.0 41.9 %layer.1 = bf16[2,64]{1,0:T(2,128)(2,1)} custom-call(bf16[2,16,128]{2,1,0:T(8,128)(2,1)} %q_hbm.1, bf16[2,1,512,128]{3,2,1,0:T(8,128)(2,1)} %k_hbm.1, bf16[2,1,512,128]{3,2,1,0:T(8,128)(2,1)} %v_hbm.1, bf16[2,128]{1,0:T(2,128)(2,1)} %bitcast.2, bf16[2,128]{1,0:T(2,128)(2,1)} %bitcast.3, s32[2]{0:T(128)} %len_hbm.1, bf16[2,64]{1,0:T(2,128)(2,1)} %res_hbm.1, ...), custom_call_target="tpu_custom_call" | custom-call | tf_op jit(solution)/shard_map/layer/pallas_call | solution.py:309
  41.9 1.2 %copy.14 = bf16[2,64]{1,0:T(2,128)(2,1)} copy(bf16[2,64]{1,0:T(2,128)(2,1)} %layer.1) | data formatting | bytes 512

commit v3 on v2

--- a/solution.py
+++ b/solution.py
@@ -30,7 +30,7 @@
     q_hbm, k_hbm, v_hbm, nk_hbm, nv_hbm, len_hbm, res_hbm, wo_hbm, gain_hbm, wg_hbm, wu_hbm, wd_hbm,
     out_ref,
     q_ref, nk_ref, nv_ref, len_ref, res_ref, gain_ref,
-    k_buf, v_buf, wo_buf, wg_buf, wu_buf, wd_buf,
+    k_buf, v_buf, wo_buf, wgu_buf, wd_buf,
     y_acc, y_stat, z_acc, z_stat, att_buf,
     gain_buf, e_buf, stream_buf, f_buf, h_send, h_buf, i_send, i_buf,
     local_sem, y_send_sem, y_recv_sem, z_send_sem, z_recv_sem, ys_send_sem, ys_recv_sem, zs_send_sem, zs_recv_sem,
@@ -52,11 +52,6 @@
     z_peers = [(at_yz(y, lax.rem(z + d, NZ))) for d in (4, 3, 5, 2, 6, 1, 7)]
     head_offsets = [(2, 1), (2, 0), (1, 1), (3, 1), (1, 0), (3, 0), (0, 1)]
     head_peers = [lax.rem(x + dx, NX) * NC + lax.rem(core + dc, NC) for dx, dc in head_offsets]
-
-    barrier = pltpu.get_barrier_semaphore()
-    greeted = z_peers + [at_head(hh) for hh in head_peers] + y_peers
-    for peer in greeted:
-        pl.semaphore_signal(barrier, inc=1, device_id=peer, device_id_type=MESH)
 
     smalls = [
         pltpu.make_async_copy(src, dst, small_sem.at[i])
@@ -72,11 +67,16 @@
         loads.append(pltpu.make_async_copy(k_hbm.at[b, 0], k_buf.at[b], local_sem.at[b]))
         loads.append(pltpu.make_async_copy(v_hbm.at[b, 0], v_buf.at[b], local_sem.at[2 + b]))
     load_wo = pltpu.make_async_copy(wo_hbm, wo_buf, local_sem.at[4])
-    load_wg = pltpu.make_async_copy(wg_hbm, wg_buf, local_sem.at[5])
-    load_wu = pltpu.make_async_copy(wu_hbm, wu_buf, local_sem.at[6])
+    load_wg = pltpu.make_async_copy(wg_hbm, wgu_buf.at[pl.ds(0, UNITS)], local_sem.at[5])
+    load_wu = pltpu.make_async_copy(wu_hbm, wgu_buf.at[pl.ds(128, UNITS)], local_sem.at[6])
     load_wd = pltpu.make_async_copy(wd_hbm, wd_buf, local_sem.at[7])
-    for load in smalls[:1] + loads + smalls[1:] + [load_wo, load_wg, load_wu, load_wd]:
+    for load in smalls[:1] + loads + smalls[1:]:
         load.start()
+
+    barrier = pltpu.get_barrier_semaphore()
+    greeted = z_peers + [at_head(hh) for hh in head_peers] + y_peers
+    for peer in greeted:
+        pl.semaphore_signal(barrier, inc=1, device_id=peer, device_id_type=MESH)
 
     def put(src, dst, send_sem, recv_sem, peer):
         pltpu.make_async_remote_copy(
@@ -97,15 +97,16 @@
     def to_row(column):
         return jnp.sum(jnp.where(diagonal, column, 0.0), axis=0, keepdims=True)
 
-    for small in smalls:
+    for small in smalls + loads:
         small.wait()
+    for load in (load_wo, load_wg, load_wu, load_wd):
+        load.start()
 
     gain_mine = jnp.reshape(gain_ref[...], (1, 64))
     gain_buf[head] = jnp.where(my_half, jnp.concatenate([gain_mine, gain_mine], axis=1), 0.0)
 
     def local_attention(b):
         q = q_ref[b]
-        loads[2 * b].wait()
         scores = lax.dot_general(q, k_buf[b], NT, preferred_element_type=f32) * SCALE
         positions = kvp * TOKENS + lax.broadcasted_iota(jnp.int32, (GROUP, TOKENS), 1)
         in_range = positions < len_ref[b]
@@ -117,7 +118,6 @@
         weights = jnp.where(in_range, jnp.exp(scores - top), 0.0)
         fresh_weight = jnp.where(first, jnp.exp(fresh - top), 0.0)
         total = jnp.sum(weights, axis=1, keepdims=True) + fresh_weight
-        loads[2 * b + 1].wait()
         acc = jnp.dot(weights.astype(bf16), v_buf[b], preferred_element_type=f32)
         acc = acc + fresh_weight.astype(bf16).astype(f32) * nv_ref[b : b + 1, :].astype(f32)
         return acc, to_row(top), to_row(total)
@@ -216,29 +216,27 @@
     load_wu.wait()
 
     def gate_up(zz, carry):
-        gate, up, squares = carry
+        acts, squares = carry
         for yy in range(NY):
             block = zz * NY + yy
             part = jnp.concatenate([f_buf[block, t] for t in range(TILES)], axis=1)
             columns = pl.ds(pl.multiple_of((yy * NZ + zz) * BLOCK, BLOCK), BLOCK)
-            gate = gate + lax.dot_general(part, wg_buf[:, columns], NT, preferred_element_type=f32)
-            up = up + lax.dot_general(part, wu_buf[:, columns], NT, preferred_element_type=f32)
+            acts = acts + lax.dot_general(part, wgu_buf[:, columns], NT, preferred_element_type=f32)
             squares = squares + f_buf[block, TILES].astype(f32)
-        return gate, up, squares
-
-    zero = jnp.zeros((SEQS, UNITS), f32)
+        return acts, squares
+
     drain(f_buf.at[pl.ds(0, NY - 1)], f_recv_sem.at[z])
-    carry = gate_up(z, (zero, zero, jnp.zeros((SEQS, 128), f32)))
+    carry = gate_up(z, (jnp.zeros((SEQS, 256), f32), jnp.zeros((SEQS, 128), f32)))
 
     def gate_up_group(i, carry):
         zz = lax.rem(z + far_first(NZ - 1 - i), NZ)
         drain(f_buf.at[pl.ds(0, NY)], f_recv_sem.at[zz])
         return gate_up(zz, carry)
 
-    gate, up, squares = lax.fori_loop(1, NZ, gate_up_group, carry)
+    acts, squares = lax.fori_loop(1, NZ, gate_up_group, carry)
     factor = lax.rsqrt(jnp.sum(squares, axis=1, keepdims=True) / D + EPSILON)
-    gate = gate * factor
-    up = up * factor
+    gate = acts[:, :UNITS] * factor
+    up = acts[:, 128 : 128 + UNITS] * factor
     hidden = (gate / (1.0 + jnp.exp(-gate)) * up).astype(bf16)
 
     load_wd.wait()
@@ -253,7 +251,7 @@
 
     def send_h(yy, zz):
         block = zz * NY + yy
-        put(h_send.at[block], h_buf.at[slot], h_send_sem, h_recv_sem, at_yz(yy, zz))
+        put(h_send.at[block], h_buf.at[slot], h_send_sem, h_recv_sem.at[z], at_yz(yy, zz))
 
     def down_group(g, carry):
         zz = lax.rem(z + far_first(g), NZ)
@@ -270,13 +268,20 @@
     down(y, z)
     for t in range(TILES):
         h_buf[slot, t] = h_send[slot, t]
-    drain(h_buf.at[pl.ds(0, KVP - 1)], h_recv_sem)
-
-    def add_block(s, sums):
-        return tuple(sums[t] + h_buf[s, t].astype(f32) for t in range(TILES))
-
-    sums = tuple(jnp.zeros((SEQS, 128), f32) for _ in range(TILES))
-    sums = lax.fori_loop(0, KVP, add_block, sums, unroll=8)
+
+    def add_blocks(zz, sums):
+        for yy in range(NY):
+            sums = tuple(sums[t] + h_buf[zz * NY + yy, t].astype(f32) for t in range(TILES))
+        return sums
+
+    def add_group(i, sums):
+        zz = lax.rem(z + far_first(NZ - 1 - i), NZ)
+        drain(h_buf.at[pl.ds(0, NY)], h_recv_sem.at[zz])
+        return add_blocks(zz, sums)
+
+    drain(h_buf.at[pl.ds(0, NY - 1)], h_recv_sem.at[z])
+    sums = add_blocks(z, tuple(jnp.zeros((SEQS, 128), f32) for _ in range(TILES)))
+    sums = lax.fori_loop(1, NZ, add_group, sums)
     for t in range(TILES):
         i_send[t] = sums[t]
 
@@ -308,7 +313,7 @@
     dma = pltpu.SemaphoreType.DMA
     return pl.pallas_call(
         kernel,
-        out_shape=jax.ShapeDtypeStruct((SEQS, D // KVP // HEAD), bf16),
+        out_shape=pltpu.VMEM((SEQS, D // KVP // HEAD), bf16),
         in_specs=[hbm] * 12,
         out_specs=vmem,
         scratch_shapes=[
@@ -321,8 +326,7 @@
             pltpu.VMEM((SEQS, TOKENS, HD), bf16),
             pltpu.VMEM((SEQS, TOKENS, HD), bf16),
             pltpu.VMEM((GROUP * HD, BLOCK), bf16),
-            pltpu.VMEM((UNITS, D), bf16),
-            pltpu.VMEM((UNITS, D), bf16),
+            pltpu.VMEM((256, D), bf16),
             pltpu.VMEM((UNITS, D), bf16),
             pltpu.VMEM((SEQS, NY, GROUP, HD), bf16),
             pltpu.VMEM((SEQS, NY, 2, 128), f32),
@@ -340,10 +344,10 @@
             dma((8,)),
             dma((SEQS,)), dma((SEQS,)), dma((SEQS,)), dma((SEQS,)),
             dma((SEQS,)), dma((SEQS,)), dma((SEQS,)), dma((SEQS,)),
-            dma, dma, dma, dma, dma, dma((NZ,)), dma, dma, dma, dma, dma((6,)),
+            dma, dma, dma, dma, dma, dma((NZ,)), dma, dma((NZ,)), dma, dma, dma((6,)),
         ],
         compiler_params=pltpu.CompilerParams(
-            collective_id=0, has_side_effects=True, vmem_limit_bytes=64 * 1024 * 1024
+            collective_id=0, has_side_effects=True, vmem_limit_bytes=62 * 1024 * 1024
         ),
         name="layer",
     )(*args)

time: 43.2 us -> 40.2 us (0.931)
  Pallas kernels: 41.9 us -> 39.6 us
  local copies, waits for them, and re-layouts: 1.19 us -> 0.51 us
    pallas_call x1, Pallas kernels: 41.9 us -> 39.6 us  [per_device(): pl.pallas_call(kernel, out_shape=pltpu.VMEM((SEQS, D // KVP // HEAD), bf1...]
    unnamed x1, local copies, waits for them, and re-layouts: 1.19 us -> 0.51 us
where the time goes in v3:
time: 40.2 us; the launch traced here: 40.1 us
  Pallas kernels  39.6 us (99%)
  local copies, waits for them, and re-layouts  0.51 us (1%)
    pallas_call x1, Pallas kernels, per_device(): pl.pallas_call(kernel, out_shape=pltpu.VMEM((SEQS, D // KVP // HEAD), bf1...  39.6 us

profile of v3, /device:TPU:1, one launch (start us, length us, event | category | flops | bytes accessed | tf_op | source)
XLA Modules:
  0.0 40.1 jit_solution(5779255446816997676)
XLA Ops:
  0.0 39.6 %layer.1 = bf16[2,64]{1,0:T(2,128)(2,1)S(1)} custom-call(bf16[2,16,128]{2,1,0:T(8,128)(2,1)} %q_hbm.1, bf16[2,1,512,128]{3,2,1,0:T(8,128)(2,1)} %k_hbm.1, bf16[2,1,512,128]{3,2,1,0:T(8,128)(2,1)} %v_hbm.1, bf16[2,128]{1,0:T(2,128)(2,1)} %bitcast.2, bf16[2,128]{1,0:T(2,128)(2,1)} %bitcast.3, s32[2]{0:T(128)} %len_hbm.1, bf16[2,64]{1,0:T(2,128)(2,1)} %res_hbm.1, ...), custom_call_target="tpu_custom_call" | custom-call | tf_op jit(solution)/shard_map/layer/pallas_call | solution.py:314
  39.6 0.5 %copy.14 = bf16[2,64]{1,0:T(2,128)(2,1)} copy(bf16[2,64]{1,0:T(2,128)(2,1)S(1)} %layer.1) | data formatting | bytes 512

commit v4 on v3

--- a/solution.py
+++ b/solution.py
@@ -26,13 +26,24 @@
     return jnp.where(lax.rem(g, 2) == 1, 4 - (g + 1) // 2, 4 + g // 2)
 
 
+def packed(offsets):
+    return sum(offset << (3 * i) for i, offset in enumerate(offsets))
+
+
+SENT, USED = packed((4, 1, 7, 2, 6, 3, 5)), packed((1, 7, 0, 2, 6, 4, 3, 5))
+
+
+def nth(offsets, i):
+    return jnp.bitwise_and(lax.shift_right_logical(jnp.int32(offsets), jnp.int32(3 * i)), 7)
+
+
 def kernel(
     q_hbm, k_hbm, v_hbm, nk_hbm, nv_hbm, len_hbm, res_hbm, wo_hbm, gain_hbm, wg_hbm, wu_hbm, wd_hbm,
     out_ref,
     q_ref, nk_ref, nv_ref, len_ref, res_ref, gain_ref,
-    k_buf, v_buf, wo_buf, wgu_buf, wd_buf,
+    k_buf, v_buf, wo_buf, wgu_buf, wt_buf, wd_buf,
     y_acc, y_stat, z_acc, z_stat, att_buf,
-    gain_buf, e_buf, stream_buf, f_buf, h_send, h_buf, i_send, i_buf,
+    gain_buf, e_buf, stream_buf, f_buf, f_own, h_send, h_buf, i_send, i_buf,
     local_sem, y_send_sem, y_recv_sem, z_send_sem, z_recv_sem, ys_send_sem, ys_recv_sem, zs_send_sem, zs_recv_sem,
     gain_send_sem, gain_recv_sem, e_send_sem, e_recv_sem, f_send_sem, f_recv_sem, h_send_sem, h_recv_sem,
     i_send_sem, i_recv_sem, small_sem,
@@ -48,10 +59,34 @@
     def at_head(hh):
         return (kvp, hh)
 
-    y_peers = [(at_yz(lax.rem(y + d, NY), z)) for d in (2, 1, 3)]
-    z_peers = [(at_yz(y, lax.rem(z + d, NZ))) for d in (4, 3, 5, 2, 6, 1, 7)]
-    head_offsets = [(2, 1), (2, 0), (1, 1), (3, 1), (1, 0), (3, 0), (0, 1)]
-    head_peers = [lax.rem(x + dx, NX) * NC + lax.rem(core + dc, NC) for dx, dc in head_offsets]
+    def y_peer(i):
+        return at_yz(lax.rem(y + jnp.where(lax.rem(i, 2) == 1, 2 - (i + 1) // 2, 2 + i // 2), NY), z)
+
+    def z_peer(i):
+        return at_yz(y, lax.rem(z + far_first(i), NZ))
+
+    def head_peer(i):
+        pair = i // NC
+        dx = jnp.where(lax.rem(pair, 2) == 1, 2 - (pair + 1) // 2, 2 + pair // 2)
+        return lax.rem(x + dx, NX), lax.rem(core + 1 - lax.rem(i, NC), NC)
+
+    def each(n, body):
+        for i in range(n):
+            body(i)
+
+    def every(n, body):
+        def step(i, carry):
+            body(i)
+            return carry
+
+        lax.fori_loop(0, n, step, 0)
+
+    def to_heads(body, loop=False):
+        def one(i):
+            xx, cc = head_peer(i)
+            body(xx, at_head(xx * NC + cc))
+
+        (every if loop else each)(HEAD - 1, one)
 
     smalls = [
         pltpu.make_async_copy(src, dst, small_sem.at[i])
@@ -69,14 +104,18 @@
     load_wo = pltpu.make_async_copy(wo_hbm, wo_buf, local_sem.at[4])
     load_wg = pltpu.make_async_copy(wg_hbm, wgu_buf.at[pl.ds(0, UNITS)], local_sem.at[5])
     load_wu = pltpu.make_async_copy(wu_hbm, wgu_buf.at[pl.ds(128, UNITS)], local_sem.at[6])
-    load_wd = pltpu.make_async_copy(wd_hbm, wd_buf, local_sem.at[7])
+    load_wd0 = pltpu.make_async_copy(wd_hbm.at[:, pl.ds(0, D // 2)], wd_buf.at[pl.ds(0, UNITS)], local_sem.at[7])
+    load_wd1 = pltpu.make_async_copy(wd_hbm.at[:, pl.ds(D // 2, D // 2)], wd_buf.at[pl.ds(128, UNITS)], local_sem.at[8])
+    barrier = pltpu.get_barrier_semaphore()
+    def greet(peer):
+        pl.semaphore_signal(barrier, inc=1, device_id=peer, device_id_type=MESH)
+
+    every(NZ - 1, lambda i: greet(z_peer(i)))
+    to_heads(lambda xx, peer: greet(peer), True)
+    every(NY - 1, lambda i: greet(y_peer(i)))
+
     for load in smalls[:1] + loads + smalls[1:]:
         load.start()
-
-    barrier = pltpu.get_barrier_semaphore()
-    greeted = z_peers + [at_head(hh) for hh in head_peers] + y_peers
-    for peer in greeted:
-        pl.semaphore_signal(barrier, inc=1, device_id=peer, device_id_type=MESH)
 
     def put(src, dst, send_sem, recv_sem, peer):
         pltpu.make_async_remote_copy(
@@ -99,7 +138,7 @@
 
     for small in smalls + loads:
         small.wait()
-    for load in (load_wo, load_wg, load_wu, load_wd):
+    for load in (load_wg, load_wu, load_wo, load_wd0, load_wd1):
         load.start()
 
     gain_mine = jnp.reshape(gain_ref[...], (1, 64))
@@ -125,16 +164,24 @@
     def send_y(b, acc, top, total):
         y_acc[b, y] = acc.astype(bf16)
         y_stat[b, y] = jnp.concatenate([top, total], axis=0)
-        for peer in y_peers:
+
+        def send(i):
+            peer = y_peer(i)
             put(y_stat.at[b, y], y_stat.at[b, y], ys_send_sem.at[b], ys_recv_sem.at[b], peer)
             put(y_acc.at[b, y], y_acc.at[b, y], y_send_sem.at[b], y_recv_sem.at[b], peer)
+
+        each(NY - 1, send)
 
     def send_z(b, acc, top, total):
         z_acc[b, z] = acc.astype(bf16)
         z_stat[b, z] = jnp.concatenate([top, total], axis=0)
-        for peer in z_peers:
+
+        def send(i):
+            peer = z_peer(i)
             put(z_stat.at[b, z], z_stat.at[b, z], zs_send_sem.at[b], zs_recv_sem.at[b], peer)
             put(z_acc.at[b, z], z_acc.at[b, z], z_send_sem.at[b], z_recv_sem.at[b], peer)
+
+        each(NZ - 1, send)
 
     def merge(n, b, acc_buf, stat_buf, acc_sem, stat_sem, last):
         drain(stat_buf.at[b, pl.ds(0, n - 1)], stat_sem.at[b])
@@ -157,15 +204,32 @@
         acc = jnp.dot(spread[:, : n * GROUP], stacked, preferred_element_type=f32)
         return acc, top, total
 
+    def turn(first, last):
+        def block(i, carry):
+            columns = pl.ds(pl.multiple_of(i * BLOCK, BLOCK), BLOCK)
+            wt_buf[columns, :] = wgu_buf[:, columns].T
+            return carry
+
+        lax.fori_loop(first, last, block, 0)
+
     part0 = local_attention(0)
     part1 = local_attention(1)
 
-    pl.semaphore_wait(barrier, len(greeted))
+    pl.semaphore_wait(barrier, NZ + HEAD + NY - 3)
     send_y(0, *part0)
     send_z(1, *part1)
-    for hh in head_peers:
-        put(gain_buf.at[head], gain_buf.at[head], gain_send_sem, gain_recv_sem, at_head(hh))
-
+    to_heads(lambda xx, peer: put(gain_buf.at[head], gain_buf.at[head], gain_send_sem, gain_recv_sem, peer))
+
+
+    def clear(i):
+        columns = pl.ds(pl.multiple_of(i * BLOCK, BLOCK), BLOCK)
+        for first in (UNITS, 128 + UNITS):
+            wd_buf[first : first + 128 - UNITS, columns] = jnp.zeros((128 - UNITS, BLOCK), bf16)
+
+    every(KVP // 2, clear)
+    load_wg.wait()
+    load_wu.wait()
+    turn(0, 10)
     send_z(0, *merge(NY, 0, y_acc, y_stat, y_recv_sem, ys_recv_sem, False))
     send_y(1, *merge(NZ, 1, z_acc, z_stat, z_recv_sem, zs_recv_sem, False))
     att_buf[0] = merge(NZ, 0, z_acc, z_stat, z_recv_sem, zs_recv_sem, True)[0]
@@ -178,8 +242,8 @@
     residual = jnp.where(my_half, jnp.concatenate([residual, residual], axis=1), 0.0)
     for t in range(TILES):
         e_buf[head, t] = projected[:, t * 128 : (t + 1) * 128] + jnp.where(x == t, residual, 0.0)
-    for hh in head_peers:
-        put(e_buf.at[head], e_buf.at[head], e_send_sem, e_recv_sem, at_head(hh))
+    to_heads(lambda xx, peer: put(e_buf.at[head], e_buf.at[head], e_send_sem, e_recv_sem, peer))
+    turn(10, KVP)
     drain(gain_buf.at[pl.ds(0, HEAD - 1)], gain_recv_sem)
     gains = [gain_buf[2 * t] + gain_buf[2 * t + 1] for t in range(TILES)]
     drain(e_buf.at[pl.ds(0, HEAD - 1)], e_recv_sem)
@@ -203,17 +267,16 @@
         put(f_buf.at[slot], f_buf.at[slot], f_send_sem, f_recv_sem.at[z], peer)
 
     def send_f_group(g, carry):
-        zz = lax.rem(z + far_first(g), NZ)
+        zz = lax.rem(z + nth(SENT, g), NZ)
         for dy in (2, 1, 3, 0):
             send_f(at_yz(lax.rem(y + dy, NY), zz))
         return carry
 
+    own_block = pltpu.make_async_copy(f_buf.at[slot], f_own, f_recv_sem.at[z])
+    own_block.start()
     lax.fori_loop(0, NZ - 1, send_f_group, 0)
     for dy in (2, 1, 3):
         send_f(at_yz(lax.rem(y + dy, NY), z))
-
-    load_wg.wait()
-    load_wu.wait()
 
     def gate_up(zz, carry):
         acts, squares = carry
@@ -221,51 +284,53 @@
             block = zz * NY + yy
             part = jnp.concatenate([f_buf[block, t] for t in range(TILES)], axis=1)
             columns = pl.ds(pl.multiple_of((yy * NZ + zz) * BLOCK, BLOCK), BLOCK)
-            acts = acts + lax.dot_general(part, wgu_buf[:, columns], NT, preferred_element_type=f32)
+            acts = acts + jnp.dot(part, wt_buf[columns, :], preferred_element_type=f32)
             squares = squares + f_buf[block, TILES].astype(f32)
         return acts, squares
 
-    drain(f_buf.at[pl.ds(0, NY - 1)], f_recv_sem.at[z])
-    carry = gate_up(z, (jnp.zeros((SEQS, 256), f32), jnp.zeros((SEQS, 128), f32)))
-
     def gate_up_group(i, carry):
-        zz = lax.rem(z + far_first(NZ - 1 - i), NZ)
+        zz = lax.rem(z + NZ - nth(USED, i), NZ)
         drain(f_buf.at[pl.ds(0, NY)], f_recv_sem.at[zz])
         return gate_up(zz, carry)
 
-    acts, squares = lax.fori_loop(1, NZ, gate_up_group, carry)
+    carry = (jnp.zeros((SEQS, 256), f32), jnp.zeros((SEQS, 128), f32))
+    acts, squares = lax.fori_loop(0, NZ, gate_up_group, carry)
     factor = lax.rsqrt(jnp.sum(squares, axis=1, keepdims=True) / D + EPSILON)
-    gate = acts[:, :UNITS] * factor
-    up = acts[:, 128 : 128 + UNITS] * factor
-    hidden = (gate / (1.0 + jnp.exp(-gate)) * up).astype(bf16)
-
-    load_wd.wait()
-
-    def down(yy, zz):
-        block = zz * NY + yy
-        columns = pl.ds(pl.multiple_of((yy * NZ + zz) * BLOCK, BLOCK), BLOCK)
-        part = jnp.dot(hidden, wd_buf[:, columns], preferred_element_type=f32).astype(bf16)
-        for t in range(TILES):
-            h_send[block, t] = part[:, t * 128 : (t + 1) * 128]
-        return block
+    gate = acts[:, :128] * factor
+    up = acts[:, 128:] * factor
+    hidden = jnp.where(lane < UNITS, gate / (1.0 + jnp.exp(-gate)) * up, 0.0)
+    zeros = jnp.zeros((SEQS, 128), f32)
+    hidden = jnp.concatenate(
+        [jnp.concatenate([hidden, zeros], axis=1), jnp.concatenate([zeros, hidden], axis=1)], axis=0
+    ).astype(bf16)
+
+    load_wd0.wait()
+    load_wd1.wait()
+
+    def down(zz):
+        for yy in range(NY // 2):
+            columns = pl.ds(pl.multiple_of((yy * NZ + zz) * BLOCK, BLOCK), BLOCK)
+            part = jnp.dot(hidden, wd_buf[:, columns], preferred_element_type=f32)
+            for half in range(2):
+                for t in range(TILES):
+                    h_send[zz * NY + yy + 2 * half, t] = part[
+                        SEQS * half : SEQS * (half + 1), t * 128 : (t + 1) * 128
+                    ].astype(bf16)
 
     def send_h(yy, zz):
-        block = zz * NY + yy
-        put(h_send.at[block], h_buf.at[slot], h_send_sem, h_recv_sem.at[z], at_yz(yy, zz))
+        put(h_send.at[zz * NY + yy], h_buf.at[slot], h_send_sem, h_recv_sem.at[z], at_yz(yy, zz))
 
     def down_group(g, carry):
         zz = lax.rem(z + far_first(g), NZ)
-        for dy in (2, 1, 3, 0):
-            down(lax.rem(y + dy, NY), zz)
+        down(zz)
         for dy in (2, 1, 3, 0):
             send_h(lax.rem(y + dy, NY), zz)
         return carry
 
     lax.fori_loop(0, NZ - 1, down_group, 0)
+    down(z)
     for dy in (2, 1, 3):
-        down(lax.rem(y + dy, NY), z)
         send_h(lax.rem(y + dy, NY), z)
-    down(y, z)
     for t in range(TILES):
         h_buf[slot, t] = h_send[slot, t]
 
@@ -285,8 +350,7 @@
     for t in range(TILES):
         i_send[t] = sums[t]
 
-    for (dx, dc), hh in zip(head_offsets, head_peers):
-        put(i_send.at[lax.rem(x + dx, NX)], i_buf.at[head], i_send_sem, i_recv_sem, at_head(hh))
+    to_heads(lambda xx, peer: put(i_send.at[xx], i_buf.at[head], i_send_sem, i_recv_sem, peer))
     i_buf[head] = i_send[x]
     total = stream_buf[x]
     drain(i_buf.at[pl.ds(0, HEAD - 1)], i_recv_sem)
@@ -327,7 +391,8 @@
             pltpu.VMEM((SEQS, TOKENS, HD), bf16),
             pltpu.VMEM((GROUP * HD, BLOCK), bf16),
             pltpu.VMEM((256, D), bf16),
-            pltpu.VMEM((UNITS, D), bf16),
+            pltpu.VMEM((D, 256), bf16),
+            pltpu.VMEM((256, D // 2), bf16),
             pltpu.VMEM((SEQS, NY, GROUP, HD), bf16),
             pltpu.VMEM((SEQS, NY, 2, 128), f32),
             pltpu.VMEM((SEQS, NZ, GROUP, HD), bf16),
@@ -337,11 +402,12 @@
             pltpu.VMEM((HEAD, TILES, SEQS, 128), f32),
             pltpu.VMEM((TILES, SEQS, 128), f32),
             pltpu.VMEM((KVP, TILES + 1, SEQS, 128), bf16),
+            pltpu.VMEM((TILES + 1, SEQS, 128), bf16),
             pltpu.VMEM((KVP, TILES, SEQS, 128), bf16),
             pltpu.VMEM((KVP, TILES, SEQS, 128), bf16),
             pltpu.VMEM((TILES, SEQS, 128), f32),
             pltpu.VMEM((HEAD, SEQS, 128), f32),
-            dma((8,)),
+            dma((9,)),
             dma((SEQS,)), dma((SEQS,)), dma((SEQS,)), dma((SEQS,)),
             dma((SEQS,)), dma((SEQS,)), dma((SEQS,)), dma((SEQS,)),
             dma, dma, dma, dma, dma, dma((NZ,)), dma, dma((NZ,)), dma, dma, dma((6,)),

time: 40.2 us -> 39.2 us (0.975)
  Pallas kernels: 39.6 us -> 38.6 us
    pallas_call x1, Pallas kernels: 39.6 us -> 38.6 us  [per_device(): pl.pallas_call(kernel, out_shape=pltpu.VMEM((SEQS, D // KVP // HEAD), bf1...]
where the time goes in v4:
time: 39.2 us; the launch traced here: 39.1 us
  Pallas kernels  38.6 us (98%)
  local copies, waits for them, and re-layouts  0.51 us (1%)
    pallas_call x1, Pallas kernels, per_device(): pl.pallas_call(kernel, out_shape=pltpu.VMEM((SEQS, D // KVP // HEAD), bf1...  38.6 us

profile of v4, /device:TPU:1, one launch (start us, length us, event | category | flops | bytes accessed | tf_op | source)
XLA Modules:
  0.0 39.1 jit_solution(7727491695024886600)
XLA Ops:
  0.0 38.6 %layer.1 = bf16[2,64]{1,0:T(2,128)(2,1)S(1)} custom-call(bf16[2,16,128]{2,1,0:T(8,128)(2,1)} %q_hbm.1, bf16[2,1,512,128]{3,2,1,0:T(8,128)(2,1)} %k_hbm.1, bf16[2,1,512,128]{3,2,1,0:T(8,128)(2,1)} %v_hbm.1, bf16[2,128]{1,0:T(2,128)(2,1)} %bitcast.2, bf16[2,128]{1,0:T(2,128)(2,1)} %bitcast.3, s32[2]{0:T(128)} %len_hbm.1, bf16[2,64]{1,0:T(2,128)(2,1)} %res_hbm.1, ...), custom_call_target="tpu_custom_call" | custom-call | tf_op jit(solution)/shard_map/layer/pallas_call | solution.py:378
  38.6 0.5 %copy.14 = bf16[2,64]{1,0:T(2,128)(2,1)} copy(bf16[2,64]{1,0:T(2,128)(2,1)S(1)} %layer.1) | data formatting | bytes 512

commit v5 on v4

--- a/solution.py
+++ b/solution.py
@@ -22,8 +22,8 @@
 SCALE = HD**-0.5
 
 
-def far_first(g):
-    return jnp.where(lax.rem(g, 2) == 1, 4 - (g + 1) // 2, 4 + g // 2)
+def mod(value, n):
+    return jnp.bitwise_and(value, n - 1)
 
 
 def packed(offsets):
@@ -31,6 +31,7 @@
 
 
 SENT, USED = packed((4, 1, 7, 2, 6, 3, 5)), packed((1, 7, 0, 2, 6, 4, 3, 5))
+FAR_Z, NEAR_Z, FAR_Y = packed((4, 3, 5, 2, 6, 1, 7, 0)), packed((0, 7, 1, 6, 2, 5, 3, 4)), packed((2, 1, 3, 0))
 
 
 def nth(offsets, i):
@@ -49,8 +50,8 @@
     i_send_sem, i_recv_sem, small_sem,
 ):
     kvp, head = lax.axis_index("kvp"), lax.axis_index("head")
-    y, z = kvp // NZ, lax.rem(kvp, NZ)
-    x, core = head // NC, lax.rem(head, NC)
+    y, z = lax.shift_right_logical(kvp, 3), mod(kvp, NZ)
+    x, core = lax.shift_right_logical(head, 1), mod(head, NC)
     slot = z * NY + y
 
     def at_yz(yy, zz):
@@ -60,15 +61,14 @@
         return (kvp, hh)
 
     def y_peer(i):
-        return at_yz(lax.rem(y + jnp.where(lax.rem(i, 2) == 1, 2 - (i + 1) // 2, 2 + i // 2), NY), z)
+        return at_yz(mod(y + nth(FAR_Y, i), NY), z)
 
     def z_peer(i):
-        return at_yz(y, lax.rem(z + far_first(i), NZ))
+        return at_yz(y, mod(z + nth(FAR_Z, i), NZ))
 
     def head_peer(i):
-        pair = i // NC
-        dx = jnp.where(lax.rem(pair, 2) == 1, 2 - (pair + 1) // 2, 2 + pair // 2)
-        return lax.rem(x + dx, NX), lax.rem(core + 1 - lax.rem(i, NC), NC)
+        dx = nth(FAR_Y, i // NC if isinstance(i, int) else lax.shift_right_logical(i, 1))
+        return mod(x + dx, NX), mod(core + 1 - mod(i, NC), NC)
 
     def each(n, body):
         for i in range(n):
@@ -126,7 +126,6 @@
         pltpu.make_async_copy(ref, ref, sem).wait()
 
     lane = lax.broadcasted_iota(jnp.int32, (1, 128), 1)
-    lane16 = lax.rem(lane, GROUP)
     lane_group = lane // GROUP
     diagonal = lax.broadcasted_iota(jnp.int32, (GROUP, 128), 0) == lax.rem(
         lax.broadcasted_iota(jnp.int32, (GROUP, 128), 1), GROUP
@@ -136,13 +135,8 @@
     def to_row(column):
         return jnp.sum(jnp.where(diagonal, column, 0.0), axis=0, keepdims=True)
 
-    for small in smalls + loads:
-        small.wait()
-    for load in (load_wg, load_wu, load_wo, load_wd0, load_wd1):
-        load.start()
-
-    gain_mine = jnp.reshape(gain_ref[...], (1, 64))
-    gain_buf[head] = jnp.where(my_half, jnp.concatenate([gain_mine, gain_mine], axis=1), 0.0)
+    for load in smalls[:4] + loads:
+        load.wait()
 
     def local_attention(b):
         q = q_ref[b]
@@ -218,6 +212,13 @@
     pl.semaphore_wait(barrier, NZ + HEAD + NY - 3)
     send_y(0, *part0)
     send_z(1, *part1)
+    for load in (load_wg, load_wu, load_wo, load_wd0, load_wd1):
+        load.start()
+    for load in smalls[4:]:
+        load.wait()
+
+    gain_mine = jnp.reshape(gain_ref[...], (1, 64))
+    gain_buf[head] = jnp.where(my_half, jnp.concatenate([gain_mine, gain_mine], axis=1), 0.0)
     to_heads(lambda xx, peer: put(gain_buf.at[head], gain_buf.at[head], gain_send_sem, gain_recv_sem, peer))
 
 
@@ -226,12 +227,12 @@
         for first in (UNITS, 128 + UNITS):
             wd_buf[first : first + 128 - UNITS, columns] = jnp.zeros((128 - UNITS, BLOCK), bf16)
 
+    send_z(0, *merge(NY, 0, y_acc, y_stat, y_recv_sem, ys_recv_sem, False))
+    send_y(1, *merge(NZ, 1, z_acc, z_stat, z_recv_sem, zs_recv_sem, False))
     every(KVP // 2, clear)
     load_wg.wait()
     load_wu.wait()
-    turn(0, 10)
-    send_z(0, *merge(NY, 0, y_acc, y_stat, y_recv_sem, ys_recv_sem, False))
-    send_y(1, *merge(NZ, 1, z_acc, z_stat, z_recv_sem, zs_recv_sem, False))
+    turn(0, 12)
     att_buf[0] = merge(NZ, 0, z_acc, z_stat, z_recv_sem, zs_recv_sem, True)[0]
     att_buf[1] = merge(NY, 1, y_acc, y_stat, y_recv_sem, ys_recv_sem, True)[0]
 
@@ -243,7 +244,7 @@
     for t in range(TILES):
         e_buf[head, t] = projected[:, t * 128 : (t + 1) * 128] + jnp.where(x == t, residual, 0.0)
     to_heads(lambda xx, peer: put(e_buf.at[head], e_buf.at[head], e_send_sem, e_recv_sem, peer))
-    turn(10, KVP)
+    turn(12, KVP)
     drain(gain_buf.at[pl.ds(0, HEAD - 1)], gain_recv_sem)
     gains = [gain_buf[2 * t] + gain_buf[2 * t + 1] for t in range(TILES)]
     drain(e_buf.at[pl.ds(0, HEAD - 1)], e_recv_sem)
@@ -267,16 +268,16 @@
         put(f_buf.at[slot], f_buf.at[slot], f_send_sem, f_recv_sem.at[z], peer)
 
     def send_f_group(g, carry):
-        zz = lax.rem(z + nth(SENT, g), NZ)
+        zz = mod(z + nth(SENT, g), NZ)
         for dy in (2, 1, 3, 0):
-            send_f(at_yz(lax.rem(y + dy, NY), zz))
+            send_f(at_yz(mod(y + dy, NY), zz))
         return carry
 
     own_block = pltpu.make_async_copy(f_buf.at[slot], f_own, f_recv_sem.at[z])
     own_block.start()
     lax.fori_loop(0, NZ - 1, send_f_group, 0)
     for dy in (2, 1, 3):
-        send_f(at_yz(lax.rem(y + dy, NY), z))
+        send_f(at_yz(mod(y + dy, NY), z))
 
     def gate_up(zz, carry):
         acts, squares = carry
@@ -289,7 +290,7 @@
         return acts, squares
 
     def gate_up_group(i, carry):
-        zz = lax.rem(z + NZ - nth(USED, i), NZ)
+        zz = mod(z + NZ - nth(USED, i), NZ)
         drain(f_buf.at[pl.ds(0, NY)], f_recv_sem.at[zz])
         return gate_up(zz, carry)
 
@@ -321,43 +322,18 @@
         put(h_send.at[zz * NY + yy], h_buf.at[slot], h_send_sem, h_recv_sem.at[z], at_yz(yy, zz))
 
     def down_group(g, carry):
-        zz = lax.rem(z + far_first(g), NZ)
+        zz = mod(z + nth(FAR_Z, g), NZ)
         down(zz)
         for dy in (2, 1, 3, 0):
-            send_h(lax.rem(y + dy, NY), zz)
+            send_h(mod(y + dy, NY), zz)
         return carry
 
     lax.fori_loop(0, NZ - 1, down_group, 0)
     down(z)
     for dy in (2, 1, 3):
-        send_h(lax.rem(y + dy, NY), z)
+        send_h(mod(y + dy, NY), z)
     for t in range(TILES):
         h_buf[slot, t] = h_send[slot, t]
-
-    def add_blocks(zz, sums):
-        for yy in range(NY):
-            sums = tuple(sums[t] + h_buf[zz * NY + yy, t].astype(f32) for t in range(TILES))
-        return sums
-
-    def add_group(i, sums):
-        zz = lax.rem(z + far_first(NZ - 1 - i), NZ)
-        drain(h_buf.at[pl.ds(0, NY)], h_recv_sem.at[zz])
-        return add_blocks(zz, sums)
-
-    drain(h_buf.at[pl.ds(0, NY - 1)], h_recv_sem.at[z])
-    sums = add_blocks(z, tuple(jnp.zeros((SEQS, 128), f32) for _ in range(TILES)))
-    sums = lax.fori_loop(1, NZ, add_group, sums)
-    for t in range(TILES):
-        i_send[t] = sums[t]
-
-    to_heads(lambda xx, peer: put(i_send.at[xx], i_buf.at[head], i_send_sem, i_recv_sem, peer))
-    i_buf[head] = i_send[x]
-    total = stream_buf[x]
-    drain(i_buf.at[pl.ds(0, HEAD - 1)], i_recv_sem)
-    for hh in range(HEAD):
-        total = total + i_buf[hh]
-    out_ref[...] = jnp.where(core == 0, total[:, :64], total[:, 64:]).astype(bf16)
-
     for b in range(SEQS):
         drain(y_acc.at[b, pl.ds(0, NY - 1)], y_send_sem.at[b])
         drain(y_stat.at[b, pl.ds(0, NY - 1)], ys_send_sem.at[b])
@@ -366,6 +342,31 @@
     drain(gain_buf.at[pl.ds(0, HEAD - 1)], gain_send_sem)
     drain(e_buf.at[pl.ds(0, HEAD - 1)], e_send_sem)
     drain(f_buf.at[pl.ds(0, KVP - 1)], f_send_sem)
+
+    def add_blocks(zz, sums):
+        for yy in range(NY):
+            sums = tuple(sums[t] + h_buf[zz * NY + yy, t].astype(f32) for t in range(TILES))
+        return sums
+
+    def add_group(i, sums):
+        zz = mod(z + nth(NEAR_Z, i), NZ)
+        drain(h_buf.at[pl.ds(0, NY)], h_recv_sem.at[zz])
+        return add_blocks(zz, sums)
+
+    drain(h_buf.at[pl.ds(0, NY - 1)], h_recv_sem.at[z])
+    sums = add_blocks(z, tuple(jnp.zeros((SEQS, 128), f32) for _ in range(TILES)))
+    sums = lax.fori_loop(1, NZ, add_group, sums)
+    for t in range(TILES):
+        i_send[t] = sums[t]
+
+    to_heads(lambda xx, peer: put(i_send.at[xx], i_buf.at[head], i_send_sem, i_recv_sem, peer))
+    i_buf[head] = i_send[x]
+    total = stream_buf[x]
+    drain(i_buf.at[pl.ds(0, HEAD - 1)], i_recv_sem)
+    for hh in range(HEAD):
+        total = total + i_buf[hh]
+    out_ref[...] = jnp.where(core == 0, total[:, :64], total[:, 64:]).astype(bf16)
+
     drain(h_buf.at[pl.ds(0, KVP - 1)], h_send_sem)
     drain(i_buf.at[pl.ds(0, HEAD - 1)], i_send_sem)
 

time: 39.2 us -> 39.1 us (level)
  no operation moved by 1% of the time
where the time goes in v5:
time: 39.1 us; the launch traced here: 39 us
  Pallas kernels  38.5 us (98%)
  local copies, waits for them, and re-layouts  0.51 us (1%)
    pallas_call x1, Pallas kernels, per_device(): pl.pallas_call(kernel, out_shape=pltpu.VMEM((SEQS, D // KVP // HEAD), bf1...  38.5 us

profile of v5, /device:TPU:1, one launch (start us, length us, event | category | flops | bytes accessed | tf_op | source)
XLA Modules:
  0.0 39.0 jit_solution(3040960197755133853)
XLA Ops:
  0.0 38.5 %layer.1 = bf16[2,64]{1,0:T(2,128)(2,1)S(1)} custom-call(bf16[2,16,128]{2,1,0:T(8,128)(2,1)} %q_hbm.1, bf16[2,1,512,128]{3,2,1,0:T(8,128)(2,1)} %k_hbm.1, bf16[2,1,512,128]{3,2,1,0:T(8,128)(2,1)} %v_hbm.1, bf16[2,128]{1,0:T(2,128)(2,1)} %bitcast.2, bf16[2,128]{1,0:T(2,128)(2,1)} %bitcast.3, s32[2]{0:T(128)} %len_hbm.1, bf16[2,64]{1,0:T(2,128)(2,1)} %res_hbm.1, ...), custom_call_target="tpu_custom_call" | custom-call | tf_op jit(solution)/shard_map/layer/pallas_call | solution.py:379
  38.5 0.5 %copy.14 = bf16[2,64]{1,0:T(2,128)(2,1)} copy(bf16[2,64]{1,0:T(2,128)(2,1)S(1)} %layer.1) | data formatting | bytes 512

commit v6 on v5

--- a/solution.py
+++ b/solution.py
@@ -264,24 +264,27 @@
         lane == 0, piece0, jnp.where(lane == 1, piece1, jnp.where(lane == 2, piece2, 0.0))
     ).astype(bf16)
 
-    def send_f(peer):
-        put(f_buf.at[slot], f_buf.at[slot], f_send_sem, f_recv_sem.at[z], peer)
+    def send_f(peer, far):
+        put(f_buf.at[slot], f_buf.at[slot], f_send_sem, f_recv_sem.at[2 * z + far], peer)
 
     def send_f_group(g, carry):
         zz = mod(z + nth(SENT, g), NZ)
         for dy in (2, 1, 3, 0):
-            send_f(at_yz(mod(y + dy, NY), zz))
+            send_f(at_yz(mod(y + dy, NY), zz), dy // 2)
         return carry
 
-    own_block = pltpu.make_async_copy(f_buf.at[slot], f_own, f_recv_sem.at[z])
+    own_block = pltpu.make_async_copy(f_buf.at[slot], f_own, f_recv_sem.at[2 * z])
     own_block.start()
     lax.fori_loop(0, NZ - 1, send_f_group, 0)
     for dy in (2, 1, 3):
-        send_f(at_yz(mod(y + dy, NY), z))
+        send_f(at_yz(mod(y + dy, NY), z), dy // 2)
 
     def gate_up(zz, carry):
         acts, squares = carry
-        for yy in range(NY):
+        for dy in range(NY):
+            if dy % 2 == 0:
+                drain(f_buf.at[pl.ds(0, 2)], f_recv_sem.at[2 * zz + dy // 2])
+            yy = mod(y + NY - dy, NY)
             block = zz * NY + yy
             part = jnp.concatenate([f_buf[block, t] for t in range(TILES)], axis=1)
             columns = pl.ds(pl.multiple_of((yy * NZ + zz) * BLOCK, BLOCK), BLOCK)
@@ -291,7 +294,6 @@
 
     def gate_up_group(i, carry):
         zz = mod(z + NZ - nth(USED, i), NZ)
-        drain(f_buf.at[pl.ds(0, NY)], f_recv_sem.at[zz])
         return gate_up(zz, carry)
 
     carry = (jnp.zeros((SEQS, 256), f32), jnp.zeros((SEQS, 128), f32))
@@ -411,7 +413,7 @@
             dma((9,)),
             dma((SEQS,)), dma((SEQS,)), dma((SEQS,)), dma((SEQS,)),
             dma((SEQS,)), dma((SEQS,)), dma((SEQS,)), dma((SEQS,)),
-            dma, dma, dma, dma, dma, dma((NZ,)), dma, dma((NZ,)), dma, dma, dma((6,)),
+            dma, dma, dma, dma, dma, dma((2 * NZ,)), dma, dma((NZ,)), dma, dma, dma((6,)),
         ],
         compiler_params=pltpu.CompilerParams(
             collective_id=0, has_side_effects=True, vmem_limit_bytes=62 * 1024 * 1024

time: 39.1 us -> 40.8 us (1.043)
  Pallas kernels: 38.5 us -> 40.2 us
    pallas_call x1, Pallas kernels: 38.5 us -> 40.2 us  [per_device(): pl.pallas_call(kernel, out_shape=pltpu.VMEM((SEQS, D // KVP // HEAD), bf1...]
where the time goes in v6:
time: 40.8 us; the launch traced here: 40.7 us
  Pallas kernels  40.2 us (99%)
  local copies, waits for them, and re-layouts  0.51 us (1%)
    pallas_call x1, Pallas kernels, per_device(): pl.pallas_call(kernel, out_shape=pltpu.VMEM((SEQS, D // KVP // HEAD), bf1...  40.2 us

profile of v6, /device:TPU:1, one launch (start us, length us, event | category | flops | bytes accessed | tf_op | source)
XLA Modules:
  0.0 40.7 jit_solution(9699560719458128021)
XLA Ops:
  0.0 40.2 %layer.1 = bf16[2,64]{1,0:T(2,128)(2,1)S(1)} custom-call(bf16[2,16,128]{2,1,0:T(8,128)(2,1)} %q_hbm.1, bf16[2,1,512,128]{3,2,1,0:T(8,128)(2,1)} %k_hbm.1, bf16[2,1,512,128]{3,2,1,0:T(8,128)(2,1)} %v_hbm.1, bf16[2,128]{1,0:T(2,128)(2,1)} %bitcast.2, bf16[2,128]{1,0:T(2,128)(2,1)} %bitcast.3, s32[2]{0:T(128)} %len_hbm.1, bf16[2,64]{1,0:T(2,128)(2,1)} %res_hbm.1, ...), custom_call_target="tpu_custom_call" | custom-call | tf_op jit(solution)/shard_map/layer/pallas_call | solution.py:381
  40.2 0.5 %copy.14 = bf16[2,64]{1,0:T(2,128)(2,1)} copy(bf16[2,64]{1,0:T(2,128)(2,1)S(1)} %layer.1) | data formatting | bytes 512
